TPU v7x, 128 devices: a whole 4x4x4 slice. The times are simulated.
128 devices in a mesh: dom: 128 (over z, y, x, core).
Axes of the slice: x: 4, y: 4, z: 4, core: 2. Of those that a mesh axis runs over, the one named last changes fastest.
Arguments:
- control: float32 [1024, 2048], P('dom'), may hold values from -6 to 6
- reads: int32 [128, 4], replicated, may hold values from 0 to 1023, as said below
- neighbours: int32 [128, 4], replicated, may hold values from 0 to 127, as said below
- halo_cells: int32 [128, 4, 512], P('dom'), may hold values from 0 to 65535
- wet_mask: int32 [8388608], P('dom'), may hold values 0 or 1
- depth: float32 [8388608], P('dom'), may hold values from 1 to 2
- sensitivity: float32 [8388608], P('dom'), may hold values from -3.25 to 3.25
- obs_weight: float32 [8388608], P('dom'), may hold values from 0.2 to 2
- basis_rows: float32 [128, 4, 32, 128], P('dom'), may hold values from -1 to 1
- basis_cols: float32 [128, 4, 64, 512], P('dom'), may hold values from -0.75 to 0.75
Outputs:
- hessian_vec: float32 [1024, 2048], P('dom')
- weighted_obs: float32 [8388608], P('dom')
Inputs may be any that keep to these rules, and one draw needn't show every extreme that they name: `reads`: block b is owned by partition b // 8. Each row lists distinct blocks, in no particular order and from owners anywhere on the axis; at most 2 of a row belong to one owner, and every row has exactly 2 from one owner. `neighbours`: each row lists 4 distinct partitions other than its own; q is in row p exactly when p is in row q. `halo_cells`: local cell indices of the partition.
All inputs are finite; a program needn't handle non-finite values. No bound on the sum of `wet_mask` on one device may be relied on, other than what follows from the above.
Results may differ from a plain program's by a relative error of at most 0.000071.
Values sent between devices are 32-bit elements; how exact they have to be, the bound alone decides.
A program may use at most 64 MiB of HBM per device.

v0:
```python
import jax
import jax.numpy as jnp
from jax import lax
from jax.sharding import PartitionSpec as P

STEPS = 12


HIGH = lax.Precision.HIGHEST
KAPPA = 0.11


def patch_lap(field, wrow, wcol, rows_n, cols_n):
    grid = field.reshape(rows_n, cols_n)
    frow = wrow * (grid[:, :-1] - grid[:, 1:])
    fcol = wcol * (grid[:-1, :] - grid[1:, :])
    out = jnp.pad(frow, ((0, 0), (0, 1))) - jnp.pad(frow, ((0, 0), (1, 0)))
    out = out + jnp.pad(fcol, ((0, 1), (0, 0))) - jnp.pad(fcol, ((1, 0), (0, 0)))
    return out.reshape(-1)


def on_device(
    control,
    reads,
    neighbours,
    halo_cells,
    wet_mask,
    depth,
    sensitivity,
    obs_weight,
    basis_rows,
    basis_cols,
):
    me = lax.axis_index("dom")
    ndev = lax.axis_size("dom")
    own_n, coef_n = control.shape
    kx_n = basis_rows.shape[2]
    rows_n = basis_rows.shape[3]
    ky_n = basis_cols.shape[2]
    cols_n = basis_cols.shape[3]
    read_n = reads.shape[1]
    nbr_n = halo_cells.shape[1]
    halo_n = halo_cells.shape[2]
    my_reads = reads[me]
    everything = lax.all_gather(control, "dom", axis=0, tiled=True)
    blocks = everything[my_reads]
    coef = blocks.reshape(read_n, kx_n, ky_n)
    ux = basis_rows[0]
    uy = basis_cols[0]
    inner = jnp.einsum("rkl,rlb->rkb", coef, uy, precision=HIGH)
    bathy = jnp.einsum("rka,rkb->ab", ux, inner, precision=HIGH).reshape(-1)
    flat_cells = halo_cells[0].reshape(-1)
    row_pick = (
        flat_cells[:, None] // cols_n == jnp.arange(rows_n, dtype=jnp.int32)[None, :]
    ).astype(jnp.float32)
    col_pick = (
        flat_cells[:, None] % cols_n == jnp.arange(cols_n, dtype=jnp.int32)[None, :]
    ).astype(jnp.float32)
    nbr_me = neighbours[me]
    nbr_pick = (nbr_me[:, None] == jnp.arange(ndev, dtype=jnp.int32)[None, :]).astype(jnp.float32)

    def take_cells(field):
        lifted = jnp.dot(
            row_pick,
            field.reshape(rows_n, cols_n),
            precision=HIGH,
            preferred_element_type=jnp.float32,
        )
        return jnp.sum(lifted * col_pick, axis=1)

    def put_cells(values):
        spread = col_pick * values[:, None]
        placed = lax.dot_general(
            row_pick,
            spread,
            (((0,), (0,)), ((), ())),
            precision=HIGH,
            preferred_element_type=jnp.float32,
        )
        return placed.reshape(-1)

    def to_peers(values):
        return lax.dot_general(
            nbr_pick,
            values.reshape(nbr_n, halo_n),
            (((0,), (0,)), ((), ())),
            precision=HIGH,
            preferred_element_type=jnp.float32,
        )

    def from_peers(arrived):
        return jnp.dot(
            nbr_pick, arrived, precision=HIGH, preferred_element_type=jnp.float32
        ).reshape(-1)

    dep_cells = take_cells(depth)
    dep_in = lax.all_to_all(to_peers(dep_cells), "dom", split_axis=0, concat_axis=0, tiled=True)
    edge_w = 0.5 * (dep_cells + from_peers(dep_in))
    hgrid = depth.reshape(rows_n, cols_n)
    wrow = 0.5 * (hgrid[:, :-1] + hgrid[:, 1:])
    wcol = 0.5 * (hgrid[:-1, :] + hgrid[1:, :])
    kw = KAPPA * wet_mask.astype(jnp.float32)
    source = kw * sensitivity * bathy

    def tangent_step(step, elev):
        own_faces = take_cells(elev)
        faces_in = lax.all_to_all(
            to_peers(own_faces), "dom", split_axis=0, concat_axis=0, tiled=True
        )
        ghost = from_peers(faces_in)
        lapv = patch_lap(elev, wrow, wcol, rows_n, cols_n) + put_cells(edge_w * (own_faces - ghost))
        return elev - kw * lapv + source

    elev = lax.fori_loop(0, STEPS, tangent_step, jnp.zeros_like(bathy))
    weighted_obs = obs_weight * elev

    def adjoint_step(step, carry):
        adjoint, total = carry
        total = total + adjoint
        masked = kw * adjoint
        own_faces = take_cells(masked)
        faces_in = lax.all_to_all(
            to_peers(own_faces), "dom", split_axis=0, concat_axis=0, tiled=True
        )
        ghost = from_peers(faces_in)
        lapv = patch_lap(masked, wrow, wcol, rows_n, cols_n) + put_cells(
            edge_w * (own_faces - ghost)
        )
        return (adjoint - lapv, total)

    adjoint, total = lax.fori_loop(0, STEPS, adjoint_step, (weighted_obs, jnp.zeros_like(bathy)))
    bathy_grad = (kw * sensitivity * total).reshape(rows_n, cols_n)
    partial_value = jnp.einsum("ab,rlb->ral", bathy_grad, uy, precision=HIGH)
    coef_grad = jnp.einsum("rka,ral->rkl", ux, partial_value, precision=HIGH).reshape(
        read_n, coef_n
    )
    wanted = jnp.arange(own_n * lax.axis_size("dom"), dtype=jnp.int32)
    onehot = (my_reads[None, :] == wanted[:, None]).astype(jnp.float32)
    hessian_vec = lax.psum_scatter(
        jnp.dot(onehot, coef_grad, precision=HIGH, preferred_element_type=jnp.float32),
        "dom",
        scatter_dimension=0,
        tiled=True,
    )
    return (hessian_vec, weighted_obs)


def solution(mesh):
    return jax.shard_map(
        on_device,
        mesh=mesh,
        in_specs=(
            P("dom", None),
            P(),
            P(),
            P("dom", None, None),
            P("dom"),
            P("dom"),
            P("dom"),
            P("dom"),
            P("dom", None, None, None),
            P("dom", None, None, None),
        ),
        out_specs=(P("dom", None), P("dom")),
        check_vma=False,
    )
```

profile of v0, /device:TPU:1, one launch (start us, length us, event | category | flops | bytes accessed | tf_op | source)
XLA Modules:
  0.0 1374.5 jit_solution(18031495182201962526)
XLA Ops:
  14.5 11.5 all-to-all-start.2
  26.3 11.0 all-to-all-done.2
  37.5 47.3 %all-gather.2.cloned.1.call-done = f32[1024,2048]{1,0:T(8,128)} async-done(((f32[8,2048]{1,0:T(8,128)}), f32[1024,2048]{1,0:T(8,128)}) %all-gather.2.cloned.1.call-update) | async-done | bytes 8388624 | tf_op jit(solution)/shard_map/all_gather | solution.py:45
  90.2 310.2 %while.28 = (s32[]{:T(128)}, f32[65536]{0:T(1024)S(1)}, f32[128,511]{0,1:T(8,128)S(1)}, f32[127,512]{0,1:T(8,128)S(1)}, f32[2048]{0:T(1024)S(1)}, /*index=5*/f32...) while((s32[]{:T(128)}, f32[65536]{0:T(1024)S(1)}, ...), condition=%wide.region_3.4_spmd.clone, body=%wide.region_1.3_spmd.clone.sunk | while | flops 3234663168 | bytes 12160704 | solution.py:114
  90.3 4.3 select_reduce_fusion.5
  96.1 5.4 all-to-all-start
  102.2 10.4 all-to-all-done
  117.1 4.3 select_reduce_fusion.5
  122.8 4.4 all-to-all-start
  128.0 10.4 all-to-all-done
  142.8 4.3 select_reduce_fusion.5
  148.6 4.4 all-to-all-start
  153.8 10.4 all-to-all-done
  168.6 4.3 select_reduce_fusion.5
  174.4 4.4 all-to-all-start
  179.5 10.4 all-to-all-done
  194.4 4.3 select_reduce_fusion.5
  200.2 4.4 all-to-all-start
  205.3 10.4 all-to-all-done
  220.1 4.3 select_reduce_fusion.5
  225.9 4.4 all-to-all-start
  231.1 10.4 all-to-all-done
  245.9 4.3 select_reduce_fusion.5
  251.7 4.4 all-to-all-start
  256.8 10.4 all-to-all-done
  271.7 4.3 select_reduce_fusion.5
  277.5 4.4 all-to-all-start
  282.6 10.4 all-to-all-done
  303.2 4.4 all-to-all-start
  308.4 10.4 all-to-all-done
  329.0 4.4 all-to-all-start
  334.1 10.4 all-to-all-done
  354.8 4.4 all-to-all-start
  359.9 10.4 all-to-all-done
  374.8 4.3 select_reduce_fusion.5
  380.5 4.4 all-to-all-start
  385.7 10.4 all-to-all-done
  402.2 318.1 %while.29 = (s32[]{:T(128)}, f32[65536]{0:T(1024)S(1)}, f32[65536]{0:T(1024)}, f32[65536]{0:T(1024)S(1)}, f32[128,511]{0,1:T(8,128)S(1)}, /*index=5*/f32[127,512...) while((s32[]{:T(128)}, f32[65536]{0:T(1024)S(1)}, ...), condition=%wide.region_6.7_spmd.clone, body=%wide.region_4.6_spmd.clone.sunk | while | flops 3234597632 | bytes 14520055 | solution.py:131
  408.2 4.4 all-to-all-start.1
  413.4 10.4 all-to-all-done.1
  434.7 4.4 all-to-all-start.1
  439.9 10.4 all-to-all-done.1
  461.2 4.4 all-to-all-start.1
  466.4 10.4 all-to-all-done.1
  487.7 4.4 all-to-all-start.1
  492.9 10.4 all-to-all-done.1
  514.2 4.4 all-to-all-start.1
  519.3 10.4 all-to-all-done.1
  540.7 4.4 all-to-all-start.1
  545.8 10.4 all-to-all-done.1
  567.2 4.4 all-to-all-start.1
  572.3 10.4 all-to-all-done.1
  593.6 4.4 all-to-all-start.1
  598.8 10.4 all-to-all-done.1
  620.1 4.4 all-to-all-start.1
  625.3 10.4 all-to-all-done.1
  646.6 4.4 all-to-all-start.1
  651.8 10.4 all-to-all-done.1
  673.1 4.4 all-to-all-start.1
  678.2 10.4 all-to-all-done.1
  699.6 4.4 all-to-all-start.1
  704.7 10.4 all-to-all-done.1
  722.4 5.5 fusion.68
  728.0 639.6 %reduce-scatter.2.cloned.1.call-done = f32[8,2048]{1,0:T(8,128)} async-done(((f32[1024,2048]{1,0:T(8,128)}), f32[8,2048]{1,0:T(8,128)}) %reduce-scatter.2.cloned.1.call-update) | async-done | bytes 65552 | tf_op jit(solution)/shard_map/reduce_scatter | solution.py:139
  (597 shorter events, 246.6 us)
Async XLA Ops:
  7.2 81.8 %copy-start = (f32[1,4,64,512]{3,2,1,0:T(8,128)S(1)}, f32[1,4,64,512]{3,2,1,0:T(8,128)}, u32[]{:S(2)}) copy-start(f32[1,4,64,512]{3,2,1,0:T(8,128)} %param.23) | copy-start | bytes 1572868
  7.2 77.7 %all-gather.2.cloned.1.call-start = ((), (), s32[]{:S(2)}) async-start(), calls=%async_computation.4 | async-start | bytes 8454144 | tf_op jit(solution)/shard_map/all_gather | solution.py:45
  9.8 2.9 copy-start.8
  9.8 2.9 copy-start.9
  9.9 4.3 copy-start.3
  12.6 76.7 %copy-start.7 = (f32[1,4,32,128]{3,2,1,0:T(8,128)S(1)}, f32[1,4,32,128]{3,2,1,0:T(8,128)}, u32[]{:S(2)}) copy-start(f32[1,4,32,128]{3,2,1,0:T(8,128)} %param.22) | copy-start | bytes 196612
  12.6 77.5 %copy-start.5 = (f32[65536]{0:T(1024)S(1)}, f32[65536]{0:T(1024)}, u32[]{:S(2)}) copy-start(f32[65536]{0:T(1024)} %param.20) | copy-start | bytes 786436
  12.6 77.5 %copy-start.6 = (s32[65536]{0:T(1024)S(1)}, s32[65536]{0:T(1024)}, u32[]{:S(2)}) copy-start(s32[65536]{0:T(1024)} %param.18) | copy-start | bytes 786436
  14.5 22.8 %all-to-all-start.2 = ((f32[128,1,512]{2,1,0:T(1,128)}), f32[128,1,512]{2,1,0:T(1,128)S(1)}, u32[]{:S(2)}, u32[]{:S(2)}) async-start(f32[128,1,512]{2,1,0:T(1,128)} %copy.35), calls=%async_computation.2 | async-start | bytes 524288 | tf_op jit(solution)/shard_map/all_to_all | solution.py:97
  26.0 1341.6 %reduce-scatter.2.cloned.1.call-start = ((), (), s32[]{:S(2)}) async-start(), calls=%async_computation.5 | async-start | bytes 8454144 | tf_op jit(solution)/shard_map/reduce_scatter | solution.py:139
  96.1 16.5 %all-to-all-start = ((f32[128,1,512]{2,1,0:T(1,128)}), f32[128,1,512]{2,1,0:T(1,128)S(1)}, u32[]{:S(2)}, u32[]{:S(2)}) async-start(f32[128,1,512]{2,1,0:T(1,128)} %copy.84), calls=%async_computation | async-start | bytes 524288 | tf_op jit(solution)/shard_map/while/body/eval_jaxpr/all_to_all | solution.py:107
  122.8 15.5 %all-to-all-start = ((f32[128,1,512]{2,1,0:T(1,128)}), f32[128,1,512]{2,1,0:T(1,128)S(1)}, u32[]{:S(2)}, u32[]{:S(2)}) async-start(f32[128,1,512]{2,1,0:T(1,128)} %copy.84), calls=%async_computation | async-start | bytes 524288 | tf_op jit(solution)/shard_map/while/body/eval_jaxpr/all_to_all | solution.py:107
  148.6 15.5 %all-to-all-start = ((f32[128,1,512]{2,1,0:T(1,128)}), f32[128,1,512]{2,1,0:T(1,128)S(1)}, u32[]{:S(2)}, u32[]{:S(2)}) async-start(f32[128,1,512]{2,1,0:T(1,128)} %copy.84), calls=%async_computation | async-start | bytes 524288 | tf_op jit(solution)/shard_map/while/body/eval_jaxpr/all_to_all | solution.py:107
  174.4 15.5 %all-to-all-start = ((f32[128,1,512]{2,1,0:T(1,128)}), f32[128,1,512]{2,1,0:T(1,128)S(1)}, u32[]{:S(2)}, u32[]{:S(2)}) async-start(f32[128,1,512]{2,1,0:T(1,128)} %copy.84), calls=%async_computation | async-start | bytes 524288 | tf_op jit(solution)/shard_map/while/body/eval_jaxpr/all_to_all | solution.py:107
  200.2 15.5 %all-to-all-start = ((f32[128,1,512]{2,1,0:T(1,128)}), f32[128,1,512]{2,1,0:T(1,128)S(1)}, u32[]{:S(2)}, u32[]{:S(2)}) async-start(f32[128,1,512]{2,1,0:T(1,128)} %copy.84), calls=%async_computation | async-start | bytes 524288 | tf_op jit(solution)/shard_map/while/body/eval_jaxpr/all_to_all | solution.py:107
  225.9 15.5 %all-to-all-start = ((f32[128,1,512]{2,1,0:T(1,128)}), f32[128,1,512]{2,1,0:T(1,128)S(1)}, u32[]{:S(2)}, u32[]{:S(2)}) async-start(f32[128,1,512]{2,1,0:T(1,128)} %copy.84), calls=%async_computation | async-start | bytes 524288 | tf_op jit(solution)/shard_map/while/body/eval_jaxpr/all_to_all | solution.py:107
  251.7 15.5 %all-to-all-start = ((f32[128,1,512]{2,1,0:T(1,128)}), f32[128,1,512]{2,1,0:T(1,128)S(1)}, u32[]{:S(2)}, u32[]{:S(2)}) async-start(f32[128,1,512]{2,1,0:T(1,128)} %copy.84), calls=%async_computation | async-start | bytes 524288 | tf_op jit(solution)/shard_map/while/body/eval_jaxpr/all_to_all | solution.py:107
  277.5 15.5 %all-to-all-start = ((f32[128,1,512]{2,1,0:T(1,128)}), f32[128,1,512]{2,1,0:T(1,128)S(1)}, u32[]{:S(2)}, u32[]{:S(2)}) async-start(f32[128,1,512]{2,1,0:T(1,128)} %copy.84), calls=%async_computation | async-start | bytes 524288 | tf_op jit(solution)/shard_map/while/body/eval_jaxpr/all_to_all | solution.py:107
  303.2 15.5 %all-to-all-start = ((f32[128,1,512]{2,1,0:T(1,128)}), f32[128,1,512]{2,1,0:T(1,128)S(1)}, u32[]{:S(2)}, u32[]{:S(2)}) async-start(f32[128,1,512]{2,1,0:T(1,128)} %copy.84), calls=%async_computation | async-start | bytes 524288 | tf_op jit(solution)/shard_map/while/body/eval_jaxpr/all_to_all | solution.py:107
  329.0 15.5 %all-to-all-start = ((f32[128,1,512]{2,1,0:T(1,128)}), f32[128,1,512]{2,1,0:T(1,128)S(1)}, u32[]{:S(2)}, u32[]{:S(2)}) async-start(f32[128,1,512]{2,1,0:T(1,128)} %copy.84), calls=%async_computation | async-start | bytes 524288 | tf_op jit(solution)/shard_map/while/body/eval_jaxpr/all_to_all | solution.py:107
  354.8 15.5 %all-to-all-start = ((f32[128,1,512]{2,1,0:T(1,128)}), f32[128,1,512]{2,1,0:T(1,128)S(1)}, u32[]{:S(2)}, u32[]{:S(2)}) async-start(f32[128,1,512]{2,1,0:T(1,128)} %copy.84), calls=%async_computation | async-start | bytes 524288 | tf_op jit(solution)/shard_map/while/body/eval_jaxpr/all_to_all | solution.py:107
  380.5 15.5 %all-to-all-start = ((f32[128,1,512]{2,1,0:T(1,128)}), f32[128,1,512]{2,1,0:T(1,128)S(1)}, u32[]{:S(2)}, u32[]{:S(2)}) async-start(f32[128,1,512]{2,1,0:T(1,128)} %copy.84), calls=%async_computation | async-start | bytes 524288 | tf_op jit(solution)/shard_map/while/body/eval_jaxpr/all_to_all | solution.py:107
  401.4 0.7 copy-start.4
  408.2 15.5 %all-to-all-start.1 = ((f32[128,1,512]{2,1,0:T(1,128)}), f32[128,1,512]{2,1,0:T(1,128)S(1)}, u32[]{:S(2)}, u32[]{:S(2)}) async-start(f32[128,1,512]{2,1,0:T(1,128)} %copy.92), calls=%async_computation.1 | async-start | bytes 524288 | tf_op jit(solution)/shard_map/while/body/eval_jaxpr/all_to_all | solution.py:122
  413.2 14.8 %copy-start.1 = (f32[65536]{0:T(1024)S(1)}, f32[65536]{0:T(1024)}, u32[]{:S(2)}) copy-start(f32[65536]{0:T(1024)} %get-tuple-element.614) | copy-start | bytes 786436 | tf_op jit(solution)/shard_map/while
  428.1 0.7 copy-start.2
  434.7 15.5 %all-to-all-start.1 = ((f32[128,1,512]{2,1,0:T(1,128)}), f32[128,1,512]{2,1,0:T(1,128)S(1)}, u32[]{:S(2)}, u32[]{:S(2)}) async-start(f32[128,1,512]{2,1,0:T(1,128)} %copy.92), calls=%async_computation.1 | async-start | bytes 524288 | tf_op jit(solution)/shard_map/while/body/eval_jaxpr/all_to_all | solution.py:122
  439.7 14.8 %copy-start.1 = (f32[65536]{0:T(1024)S(1)}, f32[65536]{0:T(1024)}, u32[]{:S(2)}) copy-start(f32[65536]{0:T(1024)} %get-tuple-element.614) | copy-start | bytes 786436 | tf_op jit(solution)/shard_map/while
  454.6 0.7 copy-start.2
  461.2 15.5 %all-to-all-start.1 = ((f32[128,1,512]{2,1,0:T(1,128)}), f32[128,1,512]{2,1,0:T(1,128)S(1)}, u32[]{:S(2)}, u32[]{:S(2)}) async-start(f32[128,1,512]{2,1,0:T(1,128)} %copy.92), calls=%async_computation.1 | async-start | bytes 524288 | tf_op jit(solution)/shard_map/while/body/eval_jaxpr/all_to_all | solution.py:122
  466.1 14.8 %copy-start.1 = (f32[65536]{0:T(1024)S(1)}, f32[65536]{0:T(1024)}, u32[]{:S(2)}) copy-start(f32[65536]{0:T(1024)} %get-tuple-element.614) | copy-start | bytes 786436 | tf_op jit(solution)/shard_map/while
  481.1 0.7 copy-start.2
  487.7 15.5 %all-to-all-start.1 = ((f32[128,1,512]{2,1,0:T(1,128)}), f32[128,1,512]{2,1,0:T(1,128)S(1)}, u32[]{:S(2)}, u32[]{:S(2)}) async-start(f32[128,1,512]{2,1,0:T(1,128)} %copy.92), calls=%async_computation.1 | async-start | bytes 524288 | tf_op jit(solution)/shard_map/while/body/eval_jaxpr/all_to_all | solution.py:122
  492.6 14.8 %copy-start.1 = (f32[65536]{0:T(1024)S(1)}, f32[65536]{0:T(1024)}, u32[]{:S(2)}) copy-start(f32[65536]{0:T(1024)} %get-tuple-element.614) | copy-start | bytes 786436 | tf_op jit(solution)/shard_map/while
  507.6 0.7 copy-start.2
  514.2 15.5 %all-to-all-start.1 = ((f32[128,1,512]{2,1,0:T(1,128)}), f32[128,1,512]{2,1,0:T(1,128)S(1)}, u32[]{:S(2)}, u32[]{:S(2)}) async-start(f32[128,1,512]{2,1,0:T(1,128)} %copy.92), calls=%async_computation.1 | async-start | bytes 524288 | tf_op jit(solution)/shard_map/while/body/eval_jaxpr/all_to_all | solution.py:122
  519.1 14.8 %copy-start.1 = (f32[65536]{0:T(1024)S(1)}, f32[65536]{0:T(1024)}, u32[]{:S(2)}) copy-start(f32[65536]{0:T(1024)} %get-tuple-element.614) | copy-start | bytes 786436 | tf_op jit(solution)/shard_map/while
  534.1 0.7 copy-start.2
  540.7 15.5 %all-to-all-start.1 = ((f32[128,1,512]{2,1,0:T(1,128)}), f32[128,1,512]{2,1,0:T(1,128)S(1)}, u32[]{:S(2)}, u32[]{:S(2)}) async-start(f32[128,1,512]{2,1,0:T(1,128)} %copy.92), calls=%async_computation.1 | async-start | bytes 524288 | tf_op jit(solution)/shard_map/while/body/eval_jaxpr/all_to_all | solution.py:122
  545.6 14.8 %copy-start.1 = (f32[65536]{0:T(1024)S(1)}, f32[65536]{0:T(1024)}, u32[]{:S(2)}) copy-start(f32[65536]{0:T(1024)} %get-tuple-element.614) | copy-start | bytes 786436 | tf_op jit(solution)/shard_map/while
  560.6 0.7 copy-start.2
  567.2 15.5 %all-to-all-start.1 = ((f32[128,1,512]{2,1,0:T(1,128)}), f32[128,1,512]{2,1,0:T(1,128)S(1)}, u32[]{:S(2)}, u32[]{:S(2)}) async-start(f32[128,1,512]{2,1,0:T(1,128)} %copy.92), calls=%async_computation.1 | async-start | bytes 524288 | tf_op jit(solution)/shard_map/while/body/eval_jaxpr/all_to_all | solution.py:122
  572.1 14.8 %copy-start.1 = (f32[65536]{0:T(1024)S(1)}, f32[65536]{0:T(1024)}, u32[]{:S(2)}) copy-start(f32[65536]{0:T(1024)} %get-tuple-element.614) | copy-start | bytes 786436 | tf_op jit(solution)/shard_map/while
  587.1 0.7 copy-start.2
  593.6 15.5 %all-to-all-start.1 = ((f32[128,1,512]{2,1,0:T(1,128)}), f32[128,1,512]{2,1,0:T(1,128)S(1)}, u32[]{:S(2)}, u32[]{:S(2)}) async-start(f32[128,1,512]{2,1,0:T(1,128)} %copy.92), calls=%async_computation.1 | async-start | bytes 524288 | tf_op jit(solution)/shard_map/while/body/eval_jaxpr/all_to_all | solution.py:122
  598.6 14.8 %copy-start.1 = (f32[65536]{0:T(1024)S(1)}, f32[65536]{0:T(1024)}, u32[]{:S(2)}) copy-start(f32[65536]{0:T(1024)} %get-tuple-element.614) | copy-start | bytes 786436 | tf_op jit(solution)/shard_map/while
  613.6 0.7 copy-start.2
  620.1 15.5 %all-to-all-start.1 = ((f32[128,1,512]{2,1,0:T(1,128)}), f32[128,1,512]{2,1,0:T(1,128)S(1)}, u32[]{:S(2)}, u32[]{:S(2)}) async-start(f32[128,1,512]{2,1,0:T(1,128)} %copy.92), calls=%async_computation.1 | async-start | bytes 524288 | tf_op jit(solution)/shard_map/while/body/eval_jaxpr/all_to_all | solution.py:122
  625.1 14.8 %copy-start.1 = (f32[65536]{0:T(1024)S(1)}, f32[65536]{0:T(1024)}, u32[]{:S(2)}) copy-start(f32[65536]{0:T(1024)} %get-tuple-element.614) | copy-start | bytes 786436 | tf_op jit(solution)/shard_map/while
  640.0 0.7 copy-start.2
  646.6 15.5 %all-to-all-start.1 = ((f32[128,1,512]{2,1,0:T(1,128)}), f32[128,1,512]{2,1,0:T(1,128)S(1)}, u32[]{:S(2)}, u32[]{:S(2)}) async-start(f32[128,1,512]{2,1,0:T(1,128)} %copy.92), calls=%async_computation.1 | async-start | bytes 524288 | tf_op jit(solution)/shard_map/while/body/eval_jaxpr/all_to_all | solution.py:122
  651.5 14.8 %copy-start.1 = (f32[65536]{0:T(1024)S(1)}, f32[65536]{0:T(1024)}, u32[]{:S(2)}) copy-start(f32[65536]{0:T(1024)} %get-tuple-element.614) | copy-start | bytes 786436 | tf_op jit(solution)/shard_map/while
  666.5 0.7 copy-start.2
  673.1 15.5 %all-to-all-start.1 = ((f32[128,1,512]{2,1,0:T(1,128)}), f32[128,1,512]{2,1,0:T(1,128)S(1)}, u32[]{:S(2)}, u32[]{:S(2)}) async-start(f32[128,1,512]{2,1,0:T(1,128)} %copy.92), calls=%async_computation.1 | async-start | bytes 524288 | tf_op jit(solution)/shard_map/while/body/eval_jaxpr/all_to_all | solution.py:122
  678.0 14.8 %copy-start.1 = (f32[65536]{0:T(1024)S(1)}, f32[65536]{0:T(1024)}, u32[]{:S(2)}) copy-start(f32[65536]{0:T(1024)} %get-tuple-element.614) | copy-start | bytes 786436 | tf_op jit(solution)/shard_map/while
  693.0 0.7 copy-start.2
  699.6 15.5 %all-to-all-start.1 = ((f32[128,1,512]{2,1,0:T(1,128)}), f32[128,1,512]{2,1,0:T(1,128)S(1)}, u32[]{:S(2)}, u32[]{:S(2)}) async-start(f32[128,1,512]{2,1,0:T(1,128)} %copy.92), calls=%async_computation.1 | async-start | bytes 524288 | tf_op jit(solution)/shard_map/while/body/eval_jaxpr/all_to_all | solution.py:122
  704.5 14.8 %copy-start.1 = (f32[65536]{0:T(1024)S(1)}, f32[65536]{0:T(1024)}, u32[]{:S(2)}) copy-start(f32[65536]{0:T(1024)} %get-tuple-element.614) | copy-start | bytes 786436 | tf_op jit(solution)/shard_map/while
  719.5 0.7 copy-start.2
Sparse Core Ops, SparseCore 0:
  11.0 73.8 all-gather.1
  728.1 639.4 reduce-scatter.1
where the time goes:
time: 1380 us; the launch traced here: 1370 us
  waiting for transfers between devices  948 us (69%)
  matrix products  224 us (16%)
  starting transfers between devices  119 us (9%)
  local copies, waits for them, and re-layouts  56.6 us (4%)
  between operations  14.3 us (1%)
    reduce_scatter x1, waiting for transfers between devices, on_device(): lax.psum_scatter(jnp.dot(onehot, coef_grad, precision=HIGH, preferred_ele...  640 us
    all_to_all x12, waiting for transfers between devices, tangent_step(): lax.all_to_all(to_peers(own_faces), 'dom', split_axis=0, concat_axis=0, t...  124 us
    all_to_all x12, waiting for transfers between devices, adjoint_step(): lax.all_to_all(to_peers(own_faces), 'dom', split_axis=0, concat_axis=0, t...  124 us
    dot_general x25, matrix products, take_cells(): jnp.dot(row_pick, field.reshape(rows_n, cols_n), precision=HIGH, preferre...  106 us
    dot_general x24, matrix products, put_cells(): lax.dot_general(row_pick, spread, (((0,), (0,)), ((), ())), precision=HIG...  89.9 us
    all_to_all x12, starting transfers between devices, tangent_step(): lax.all_to_all(to_peers(own_faces), 'dom', split_axis=0, concat_axis=0, t...  54 us
    all_to_all x12, starting transfers between devices, adjoint_step(): lax.all_to_all(to_peers(own_faces), 'dom', split_axis=0, concat_axis=0, t...  53 us
    all_gather x1, waiting for transfers between devices, on_device(): everything = lax.all_gather(control, 'dom', axis=0, tiled=True)  47.3 us
  transfers between devices with their start and end apart: 27, of which 27 were waited for; matrix products, arithmetic and copies ran while one was open for 2% of the time, Pallas kernels for 0%

commit v1 on v0

v1 whole, which is shorter than its diff:
```python
import jax
import jax.numpy as jnp
from jax import lax
from jax.experimental import pallas as pl
from jax.experimental.pallas import tpu as pltpu
from jax.sharding import PartitionSpec as P

STEPS = 12
KAPPA = 0.11
HIGH = lax.Precision.HIGHEST
MESH = pl.DeviceIdType.MESH
F32 = jnp.float32
BF16 = jnp.bfloat16

NDEV = 128
LOW = 8
HIGHN = 16
ROWS, COLS = 128, 512
NB, READS, OWN = 4, 4, 8
CH = 16


def ring(d):
    return (0, 1, 2, 1)[d]


def hops(m):
    return ring((m >> 1) & 3) + ring((m >> 3) & 3) + ring((m >> 5) & 3)


FAR_FIRST = sorted(range(1, NDEV), key=lambda m: -hops(m))


def flip(value, mask, bits):
    out = value
    for i in range(bits):
        if (mask >> i) & 1:
            bit = lax.rem(lax.div(value, 1 << i), 2)
            out = out + (1 - 2 * bit) * (1 << i)
    return out


def differ(a, b, bits):
    out = 0
    for i in range(bits):
        d = lax.rem(lax.div(a, 1 << i), 2) - lax.rem(lax.div(b, 1 << i), 2)
        out = out + d * d * (1 << i)
    return out


def dot(a, b, precision=None):
    return jnp.dot(a, b, precision=precision, preferred_element_type=F32)


def halves(v):
    high = v.astype(BF16).astype(F32)
    return high, v - high


def kernel(
    tab, control, cells, wet, depth, sens, obs, brows, bcols,
    hess, wobs,
    kw, wr, wd, dia, src, bgr, ends, pick, pickt, spread, uone, uonet,
    row16, col16, uhi16, ulo16, mins, ew, kwj, xg, gx, fx, pg, sbuf, rbuf, lin,
    ph1, sb2, rb2, gr, sp, rp, wt, uall, inner, acc, kid,
    ssem, rsem, s1, r1, s2, r2, s3, r3, s4, r4,
):
    me = lax.axis_index("dom")
    my_low = lax.rem(me, LOW)
    my_high = lax.div(me, LOW)
    low_of = [flip(my_low, m, 3) for m in range(LOW)]
    high_of = [flip(my_high, m, 4) * LOW for m in range(HIGHN)]

    def peer(m):
        return high_of[m >> 3] + low_of[m & 7]

    barrier = pltpu.get_barrier_semaphore()
    for m in FAR_FIRST:
        pl.semaphore_signal(barrier, inc=1, device_id=(peer(m),), device_id_type=MESH)

    for i in range(CH):
        ph1[0:OWN, i, :] = control[:, i * 128:(i + 1) * 128]
    for k in range(NB):
        for c in range(4):
            part = cells[0, k:k + 1, c * 128:(c + 1) * 128]
            row16[4 * k + c:4 * k + c + 1, :] = lax.div(part, COLS)
            col16[4 * k + c:4 * k + c + 1, :] = lax.rem(part, COLS)
    up = lax.broadcasted_iota(jnp.int32, (ROWS, 128), 0)
    across = lax.broadcasted_iota(jnp.int32, (128, 128), 1)
    tall = lax.broadcasted_iota(jnp.int32, (COLS, 128), 0)
    for j in range(CH):
        pick[:, j * 128:(j + 1) * 128] = jnp.where(
            tall == col16[j:j + 1, :], 1.0, 0.0
        ).astype(BF16)
    nbr = [tab[READS + k, me] for k in range(NB)]
    at = [differ(nbr[k], me, 7) for k in range(NB)]
    lin[0] = jnp.zeros((4, 128), F32)

    def find_slot(q, carry):
        last = jnp.where(nbr[2] == q, 2, jnp.where(nbr[3] == q, 3, 0))
        kid[q] = jnp.where(nbr[1] == q, 1, last)
        return carry

    lax.fori_loop(0, NDEV, find_slot, 0)

    def take(field, out):
        high, low = halves(field)
        both = jnp.concatenate([high.astype(BF16), low.astype(BF16)], axis=0)
        for jj in range(CH // 2):
            lifted = dot(both, pick[:, jj * 256:(jj + 1) * 256])
            lifted = lifted[:ROWS] + lifted[ROWS:]
            for h in range(2):
                j = 2 * jj + h
                mine = jnp.where(
                    up == row16[j:j + 1, :], lifted[:, h * 128:(h + 1) * 128], 0.0
                )
                out[j:j + 1, :] = jnp.sum(mine, axis=0, keepdims=True)

    def put(values):
        high, low = halves(values)
        for j in range(CH):
            at_row = up == row16[j:j + 1, :]
            spread[0:ROWS, j * 128:(j + 1) * 128] = jnp.where(
                at_row, high[j:j + 1, :], 0.0
            ).astype(BF16)
            spread[ROWS:2 * ROWS, j * 128:(j + 1) * 128] = jnp.where(
                at_row, low[j:j + 1, :], 0.0
            ).astype(BF16)
        placed = dot(spread[...], pickt[...])
        return placed[:ROWS] + placed[ROWS:]

    few = lax.broadcasted_iota(jnp.int32, (CH, 128), 0)

    def same_cell(values):
        high, low = halves(values)
        mine = [few == uhi16[j:j + 1, :] for j in range(CH)]
        spread_h = [jnp.where(mine[j], high[j:j + 1, :], 0.0) for j in range(CH)]
        spread_l = [jnp.where(mine[j], low[j:j + 1, :], 0.0) for j in range(CH)]
        both = jnp.concatenate(
            [jnp.concatenate(spread_h, axis=1), jnp.concatenate(spread_l, axis=1)], axis=0
        ).astype(BF16)
        table = dot(both, uone[...])
        high, low = halves(table[:CH] + table[CH:])
        lifted = dot(jnp.concatenate([high, low], axis=0).astype(BF16), uonet[...])
        lifted = lifted[:CH] + lifted[CH:]
        rows = [
            jnp.sum(
                jnp.where(mine[j], lifted[:, j * 128:(j + 1) * 128], 0.0),
                axis=0,
                keepdims=True,
            )
            for j in range(CH)
        ]
        return jnp.concatenate(rows, axis=0)

    def send(values, parity):
        for k in range(NB):
            fx[k] = values[4 * k:4 * k + 4, :]
        for m in FAR_FIRST:
            there = peer(m)
            sbuf[m - 1] = fx[kid[there]]
            pltpu.make_async_remote_copy(
                sbuf.at[m - 1], rbuf.at[parity, m - 1], ssem, rsem.at[parity],
                device_id=(there,), device_id_type=MESH,
            ).start()

    def receive(parity):
        whole = pltpu.make_async_remote_copy(
            sbuf, rbuf.at[parity], ssem, rsem.at[parity],
            device_id=(peer(1),), device_id_type=MESH,
        )
        whole.wait_recv()
        lin[1:NDEV] = rbuf[parity]
        for k in range(NB):
            gx[4 * k:4 * k + 4, :] = lin[at[k]]
        whole.wait_send()

    def wait_all(sent, arrived, size, count, send_sem, recv_sem):
        pltpu.make_async_remote_copy(
            sent.at[pl.ds(size, size * count)], arrived.at[pl.ds(size, size * count)],
            send_sem, recv_sem, device_id=(peer(1),), device_id_type=MESH,
        ).wait()

    def patch(v):
        right = wr[...] * (v - pltpu.roll(v, COLS - 1, 1))
        down = wd[...] * (v - pltpu.roll(v, ROWS - 1, 0))
        return right - pltpu.roll(right, 1, 1) + down - pltpu.roll(down, 1, 0)

    def unfold(ref, c):
        return ref[pl.ds(c, ROWS, stride=4), :]

    def grid(ref):
        return jnp.concatenate([unfold(ref, c) for c in range(4)], axis=1)

    h = grid(depth)
    take(h, xg)

    pl.semaphore_wait(barrier, NDEV - 1)

    blk = OWN * CH
    first = [
        pltpu.make_async_remote_copy(
            ph1.at[pl.ds(0, OWN)], ph1.at[pl.ds(m * OWN, OWN)], s1, r1,
            device_id=(peer(m),), device_id_type=MESH,
        )
        for m in range(1, LOW)
    ]
    for copy in first:
        copy.start()
    send(xg[...], 1)

    last_col = lax.broadcasted_iota(jnp.int32, (ROWS, COLS), 1) == COLS - 1
    last_row = lax.broadcasted_iota(jnp.int32, (ROWS, COLS), 0) == ROWS - 1
    wr[...] = jnp.where(last_col, 0.0, 0.5 * (h + pltpu.roll(h, COLS - 1, 1)))
    wd[...] = jnp.where(last_row, 0.0, 0.5 * (h + pltpu.roll(h, ROWS - 1, 0)))
    mask = grid(wet).astype(F32)
    kw[...] = KAPPA * mask
    take(mask, kwj)
    kwj[...] = KAPPA * kwj[...]

    mins[...] = jnp.full((CH * 8, 128), 4096.0, F32)

    def earliest(i, carry):
        mine = row16[pl.ds(i, 1), :] * COLS + col16[pl.ds(i, 1), :]
        column = jnp.transpose(jnp.broadcast_to(mine.astype(F32), (128, 128)))
        number = (up + i * 128).astype(F32)
        for j in range(CH):
            other = (row16[j:j + 1, :] * COLS + col16[j:j + 1, :]).astype(F32)
            found = jnp.where(column == other, number, 4096.0)
            found = jnp.min(found.reshape(16, 8, 128), axis=0)
            mins[8 * j:8 * j + 8, :] = jnp.minimum(mins[8 * j:8 * j + 8, :], found)
        return carry

    lax.fori_loop(0, CH, earliest, 0)
    for j in range(CH):
        u = jnp.min(mins[8 * j:8 * j + 8, :], axis=0, keepdims=True).astype(jnp.int32)
        uhi16[j:j + 1, :] = lax.div(u, 128)
        ulo16[j:j + 1, :] = lax.rem(u, 128)
    for j in range(CH):
        ulo = ulo16[j:j + 1, :]
        uonet[:, j * 128:(j + 1) * 128] = jnp.where(up == ulo, 1.0, 0.0).astype(BF16)
        column = jnp.transpose(jnp.broadcast_to(ulo.astype(F32), (128, 128)))
        uone[j * 128:(j + 1) * 128, :] = jnp.where(
            column == across.astype(F32), 1.0, 0.0
        ).astype(BF16)
        column = jnp.transpose(
            jnp.broadcast_to(col16[j:j + 1, :].astype(F32), (128, 128))
        )
        for c in range(4):
            pickt[j * 128:(j + 1) * 128, c * 128:(c + 1) * 128] = jnp.where(
                column == (across + c * 128).astype(F32), 1.0, 0.0
            ).astype(BF16)

    wait_all(ph1, ph1, OWN, LOW - 1, s1, r1)
    part = READS * CH
    for j in range(HIGHN):
        reader = high_of[j] + my_low
        for k in range(READS):
            b = tab[k, reader]
            owner = lax.div(b, OWN)
            index = differ(lax.rem(owner, LOW), my_low, 3) * OWN + lax.rem(b, OWN)
            if j == 0:
                rb2[k] = ph1[index]
            else:
                sb2[j * READS + k] = ph1[index]
        if j:
            pltpu.make_async_remote_copy(
                sb2.at[pl.ds(j * READS, READS)], rb2.at[pl.ds(j * READS, READS)], s2, r2,
                device_id=(reader,), device_id_type=MESH,
            ).start()

    receive(1)
    ew[...] = 0.5 * (xg[...] + gx[...])
    dia[...] = put(ew[...])
    for r in range(READS):
        for p in range(2):
            uall[p * 64 + r * CH:p * 64 + (r + 1) * CH, :] = brows[
                0, r, pl.ds(p, CH, stride=2), :
            ]
    wait_all(sb2, rb2, READS, HIGHN - 1, s2, r2)

    zero = jnp.zeros((64, COLS), F32)
    for k in range(READS):
        owner = lax.div(tab[k, me], OWN)
        row = differ(lax.div(owner, LOW), my_high, 4)
        block = rb2[row * READS + k]
        uy = bcols[0, k]
        inner[k * CH:(k + 1) * CH, :] = dot(block, jnp.concatenate([uy, zero], 0), HIGH)
        inner[64 + k * CH:64 + (k + 1) * CH, :] = dot(
            block, jnp.concatenate([zero, uy], 0), HIGH
        )
    bathy = dot(jnp.transpose(uall[...]), inner[...], HIGH)
    src[...] = kw[...] * grid(sens) * bathy

    def run(phase, carry):
        s = src[...]
        bgr[...] = s
        take(s, pg)
        gx[...] = jnp.zeros((CH, 128), F32)
        fx16 = pg

        def step(n, c):
            parity = lax.rem(phase * (STEPS - 1) + n, 2)
            send(fx16[...], parity)
            k = kw[...]
            e = bgr[...] + k * put(gx[...])
            new = e - k * (patch(e) + dia[...] * e) + src[...]
            bgr[...] = new
            take(new, pg)
            receive(parity)
            x = ew[...] * gx[...]
            gx[...] = x
            pg[...] = pg[...] + kwj[...] * same_cell(x)
            return c

        lax.fori_loop(0, STEPS - 1, step, 0)
        e = bgr[...] + kw[...] * put(gx[...])
        ends[phase] = e
        src[...] = kw[...] * (grid(obs) * e)
        return carry

    lax.fori_loop(0, 2, run, 0)
    seen = grid(obs) * ends[0]
    for c in range(4):
        wobs[pl.ds(c, ROWS, stride=4), :] = seen[:, c * 128:(c + 1) * 128]

    grad = grid(sens) * ends[1]
    side = dot(uall[...], grad, HIGH)
    for r in range(READS):
        uy = bcols[0, r]
        even = lax.dot_general(
            side[r * CH:(r + 1) * CH], jnp.concatenate([uy, zero], 0),
            (((1,), (1,)), ((), ())), precision=HIGH, preferred_element_type=F32,
        )
        odd = lax.dot_general(
            side[64 + r * CH:64 + (r + 1) * CH], jnp.concatenate([zero, uy], 0),
            (((1,), (1,)), ((), ())), precision=HIGH, preferred_element_type=F32,
        )
        gr[r * CH:(r + 1) * CH, :] = even + odd

    third = [
        pltpu.make_async_remote_copy(
            gr.at[pl.ds(0, part)], gr.at[pl.ds(j * part, part)], s3, r3,
            device_id=(high_of[j] + my_low,), device_id_type=MESH,
        )
        for j in range(1, HIGHN)
    ]
    for copy in third:
        copy.start()
    lane = lax.broadcasted_iota(jnp.int32, (1, 128), 1)
    wt[...] = jnp.zeros((128, 128), F32)
    for j in range(HIGHN):
        for k in range(READS):
            b = tab[k, high_of[j] + my_low]
            owner = lax.div(b, OWN)
            index = differ(lax.rem(owner, LOW), my_low, 3) * OWN + lax.rem(b, OWN)
            index = jnp.where(lax.div(owner, LOW) == my_high, index, -1)
            s = j * READS + k
            wt[s:s + 1, :] = jnp.where(lane == index, 1.0, 0.0)
    gather = jnp.transpose(wt[...])[:64, :64]
    wait_all(gr, gr, part, HIGHN - 1, s3, r3)
    for i in range(CH):
        sp[pl.ds(i, 64, stride=CH), :] = dot(gather, gr[pl.ds(i, 64, stride=CH), :], HIGH)
    fourth = [
        pltpu.make_async_remote_copy(
            sp.at[pl.ds(m * blk, blk)], rp.at[pl.ds(m * blk, blk)], s4, r4,
            device_id=(peer(m),), device_id_type=MESH,
        )
        for m in range(1, LOW)
    ]
    for copy in fourth:
        copy.start()
    wait_all(sp, rp, blk, LOW - 1, s4, r4)
    total = sp[0:blk, :]
    for m in range(1, LOW):
        total = total + rp[m * blk:(m + 1) * blk, :]
    acc[...] = total
    for i in range(CH):
        hess[:, i * 128:(i + 1) * 128] = acc[pl.ds(i, OWN, stride=CH), :]


def on_device(
    control, reads, neighbours, halo_cells, wet_mask, depth, sensitivity, obs_weight,
    basis_rows, basis_cols,
):
    table = jnp.concatenate([reads, neighbours], axis=1).T
    flat = (ROWS * COLS // 128, 128)
    field = pltpu.VMEM((ROWS, COLS), F32)
    few = pltpu.VMEM((CH, 128), F32)
    few_int = pltpu.VMEM((CH, 128), jnp.int32)
    edges = CH * 128
    blocks = pltpu.VMEM((LOW * OWN * CH, 128), F32)
    apart = pltpu.VMEM((LOW * OWN, CH, 128), F32)
    dma = pltpu.SemaphoreType.DMA
    vmem = pl.BlockSpec(memory_space=pltpu.VMEM)
    hess, wobs = pl.pallas_call(
        kernel,
        name="hessian_product",
        out_shape=(
            jax.ShapeDtypeStruct(control.shape, F32),
            jax.ShapeDtypeStruct(flat, F32),
        ),
        in_specs=[pl.BlockSpec(memory_space=pltpu.SMEM)] + [vmem] * 8,
        out_specs=(vmem, vmem),
        scratch_shapes=[
            field, field, field, field, field, field,
            pltpu.VMEM((2, ROWS, COLS), F32),
            pltpu.VMEM((COLS, edges), BF16),
            pltpu.VMEM((edges, COLS), BF16),
            pltpu.VMEM((2 * ROWS, edges), BF16),
            pltpu.VMEM((edges, 128), BF16),
            pltpu.VMEM((128, edges), BF16),
            few_int, few_int, few_int, few_int,
            pltpu.VMEM((CH * 8, 128), F32),
            few, few, few, few,
            pltpu.VMEM((NB, 4, 128), F32),
            few,
            pltpu.VMEM((NDEV - 1, 4, 128), F32),
            pltpu.VMEM((2, NDEV - 1, 4, 128), F32),
            pltpu.VMEM((NDEV, 4, 128), F32),
            apart, apart, apart, blocks, blocks, blocks,
            pltpu.VMEM((128, 128), F32),
            pltpu.VMEM((128, 128), F32),
            pltpu.VMEM((128, COLS), F32),
            pltpu.VMEM((OWN * CH, 128), F32),
            pltpu.SMEM((NDEV,), jnp.int32),
            dma, dma((2,)), dma, dma, dma, dma, dma, dma, dma, dma,
        ],
        compiler_params=pltpu.CompilerParams(
            collective_id=0, has_side_effects=True, vmem_limit_bytes=48 << 20
        ),
    )(
        table, control, halo_cells, wet_mask.reshape(flat), depth.reshape(flat),
        sensitivity.reshape(flat), obs_weight.reshape(flat), basis_rows, basis_cols,
    )
    return hess, wobs.reshape(-1)


def solution(mesh):
    return jax.shard_map(
        on_device,
        mesh=mesh,
        in_specs=(
            P("dom", None), P(), P(), P("dom", None, None), P("dom"), P("dom"), P("dom"),
            P("dom"), P("dom", None, None, None), P("dom", None, None, None),
        ),
        out_specs=(P("dom", None), P("dom")),
        check_vma=False,
    )
```

time: 1380 us -> 227 us (0.16)
  waiting for transfers between devices: 948 us -> 0 us
  matrix products: 224 us -> 0 us
  Pallas kernels: 0 us -> 218 us
  starting transfers between devices: 119 us -> 0 us
  local copies, waits for them, and re-layouts: 56.6 us -> 7.87 us
    reduce_scatter x1 -> x0, waiting for transfers between devices: 640 us -> none  [on_device(): lax.psum_scatter(jnp.dot(onehot, coef_grad, precision=HIGH, preferred_ele...]
    all_to_all x25 -> x0, waiting for transfers between devices: 260 us -> none  [the longest x12 124 us: tangent_step(): lax.all_to_all(to_peers(own_faces), 'dom', split_axis=0, concat_axis=0, t...]
    dot_general x104 -> x0, matrix products: 224 us -> none  [the longest x25 106 us: take_cells(): jnp.dot(row_pick, field.reshape(rows_n, cols_n), precision=HIGH, preferre...]
    pallas_call x0 -> x1, Pallas kernels: none -> 218 us  [on_device(): pl.pallas_call(kernel, name='hessian_product', out_shape=(jax.ShapeDtypeS...]
    all_to_all x25 -> x0, starting transfers between devices: 119 us -> none  [the longest x12 54 us: tangent_step(): lax.all_to_all(to_peers(own_faces), 'dom', split_axis=0, concat_axis=0, t...]
    all_gather x1 -> x0, waiting for transfers between devices: 47.3 us -> none  [on_device(): everything = lax.all_gather(control, 'dom', axis=0, tiled=True)]
    all_to_all x25 -> x0, local copies, waits for them, and re-layouts: 21.1 us -> none  [the longest x12 10.1 us: adjoint_step(): lax.all_to_all(to_peers(own_faces), 'dom', split_axis=0, concat_axis=0, t...]
    while x144 -> x0, local copies, waits for them, and re-layouts: 16.6 us -> none
  transfers between devices with their start and end apart: 27 -> 0, of which waited for: 27 -> 0; matrix products, arithmetic and copies ran while one was open for 2% -> 0% of each run, Pallas kernels for 0% -> 0%
where the time goes in v1:
time: 227 us
  Pallas kernels  218 us (96%)
  local copies, waits for them, and re-layouts  7.87 us (3%)
    pallas_call x1, Pallas kernels, on_device(): pl.pallas_call(kernel, name='hessian_product', out_shape=(jax.ShapeDtypeS...  218 us
    unnamed x18, local copies, waits for them, and re-layouts  7.87 us

profile of v1, /device:TPU:1, one launch (start us, length us, event | category | flops | bytes accessed | tf_op | source)
XLA Modules:
  0.0 227.0 jit_solution(7166144670804863278)
XLA Ops:
  0.6 0.0 copy-start.7
  0.6 0.7 add_bitcast_fusion.tab
  1.4 0.0 copy-done.7
  1.4 0.0 copy-start
  1.4 1.0 copy-done
  2.4 0.0 copy-start.1
  2.4 0.9 copy-done.1
  3.3 0.0 copy-start.2
  3.4 0.9 copy-done.2
  4.3 0.0 copy-start.3
  4.3 0.9 copy-done.3
  5.2 0.0 copy-start.4
  5.3 0.9 copy-done.4
  6.2 0.0 copy-start.5
  6.2 0.8 copy-done.5
  7.0 0.0 copy-start.6
  7.0 0.8 copy-done.6
  7.9 217.8 %hessian_product.1 = (f32[8,2048]{1,0:T(8,128)S(1)}, f32[512,128]{1,0:T(8,128)S(1)}) custom-call(s32[8,128]{1,0:T(8,128)S(1)} %add_bitcast_fusion.tab, f32[8,2048]{1,0:T(8,128)S(1)} %copy-done.5, s32[1,4,512]{2,1,0:T(4,128)S(1)} %copy-done.7, s32[512,128]{1,0:T(8,128)S(1)} %bitcast.8, f32[512,128]{1,0:T(8,128)S(1)} %bitcast.9, f32[512,128]{1,0:T(8,128)S(1)} %bitcast.10, ...), custom_call_target="tpu_custom_call" | custom-call | tf_op jit(solution)/shard_map/hessian_product/pallas_call | solution.py:396
  225.6 0.6 copy.14
  226.3 0.7 copy.15
Async XLA Ops:
  0.6 0.7 copy-start.7
  1.4 1.0 copy-start
  2.4 0.9 copy-start.1
  3.3 0.9 copy-start.2
  4.3 0.9 copy-start.3
  5.2 0.9 copy-start.4
  6.2 0.8 copy-start.5
  7.0 0.8 copy-start.6

commit v2 on v1

v2 whole, which is shorter than its diff:
```python
import random

import jax
import jax.numpy as jnp
from jax import lax
from jax.experimental import pallas as pl
from jax.experimental.pallas import tpu as pltpu
from jax.sharding import PartitionSpec as P

STEPS = 12
TURN = STEPS - 1
KAPPA = 0.11
HIGH = lax.Precision.HIGHEST
MESH = pl.DeviceIdType.MESH
F32 = jnp.float32
BF16 = jnp.bfloat16

NDEV = 128
LOW = 8
HIGHN = 16
ROWS, COLS = 128, 512
NB, READS, OWN = 4, 4, 8
PIECES = 4
CH = 16
PR = CH // PIECES


def ring(d):
    return (0, 1, 2, 1)[d]


def hops(m):
    return ring((m >> 1) & 3) + ring((m >> 3) & 3) + ring((m >> 5) & 3)


def far_first():
    order = list(range(1, NDEV))
    random.Random(1).shuffle(order)
    return sorted(order, key=lambda m: -hops(m))


FAR_FIRST = far_first()


def flip(value, mask, bits):
    out = value
    for i in range(bits):
        if (mask >> i) & 1:
            bit = lax.rem(lax.div(value, 1 << i), 2)
            out = out + (1 - 2 * bit) * (1 << i)
    return out


def differ(a, b, bits):
    out = 0
    for i in range(bits):
        d = lax.rem(lax.div(a, 1 << i), 2) - lax.rem(lax.div(b, 1 << i), 2)
        out = out + d * d * (1 << i)
    return out


def dot(a, b, precision=None):
    return jnp.dot(a, b, precision=precision, preferred_element_type=F32)


def halves(v):
    high = v.astype(BF16).astype(F32)
    return high, v - high


def kernel(
    reads, nbrs, control_hbm, cells_hbm, wet_hbm, depth_hbm, sens_hbm, obs_hbm,
    brows_hbm, bcols_hbm,
    hess, wobs,
    control, cells, wet, depth, sens, obs, brows, bcols, insem,
    kw, wr, wd, dia, src, bgr, wgt, obj, seen, pick, pickt, spread, uone,
    row16, col16, uhi16, ulo16, mins, ew, kwj, xg, gx, fx, pg, sbuf, rbuf0, rbuf1,
    ph1a, ph1b, ph1c, ph1d, sb2, rb2, gr, sp, rp, wt, uall, acc, kid,
    ssem, rsem, s1, r1, s2, r2, s3, r3, s4, r4,
):
    names = (control, cells, depth, wet, brows, bcols, sens, obs)
    sources = (
        control_hbm, cells_hbm, depth_hbm, wet_hbm, brows_hbm, bcols_hbm, sens_hbm, obs_hbm
    )
    loads = [
        pltpu.make_async_copy(a, b, insem.at[i])
        for i, (a, b) in enumerate(zip(sources, names))
    ]
    for load in loads:
        load.start()
    me = lax.axis_index("dom")
    my_low = lax.rem(me, LOW)
    my_high = lax.div(me, LOW)
    low_of = [flip(my_low, m, 3) for m in range(LOW)]
    high_of = [flip(my_high, m, 4) * LOW for m in range(HIGHN)]

    def peer(m):
        return high_of[m >> 3] + low_of[m & 7]

    barrier = pltpu.get_barrier_semaphore()
    for m in FAR_FIRST:
        pl.semaphore_signal(barrier, inc=1, device_id=(peer(m),), device_id_type=MESH)

    ph1 = (ph1a, ph1b, ph1c, ph1d)
    loads[0].wait()
    loads[1].wait()
    for i in range(CH):
        ph1[i // PR][0:OWN, i % PR, :] = control[:, i * 128:(i + 1) * 128]
    for k in range(NB):
        for c in range(4):
            part = cells[0, k:k + 1, c * 128:(c + 1) * 128]
            row16[4 * k + c:4 * k + c + 1, :] = lax.div(part, COLS)
            col16[4 * k + c:4 * k + c + 1, :] = lax.rem(part, COLS)
    up = lax.broadcasted_iota(jnp.int32, (ROWS, 128), 0)
    across = lax.broadcasted_iota(jnp.int32, (128, 128), 1)
    tall = lax.broadcasted_iota(jnp.int32, (COLS, 128), 0)
    for j in range(CH):
        pick[:, j * 128:(j + 1) * 128] = jnp.where(
            tall == col16[j:j + 1, :], 1.0, 0.0
        ).astype(BF16)
    nbr = [nbrs[k, me] for k in range(NB)]
    at = [differ(nbr[k], me, 7) for k in range(NB)]
    landing = (rbuf0, rbuf1)
    for buf in landing:
        buf[0] = jnp.zeros((4, 128), F32)

    def find_slot(q, carry):
        last = jnp.where(nbr[2] == q, 2, jnp.where(nbr[3] == q, 3, 0))
        kid[q] = jnp.where(nbr[1] == q, 1, last)
        return carry

    lax.fori_loop(0, NDEV, find_slot, 0)

    def take(field, out):
        high, low = halves(field)
        both = jnp.concatenate([high.astype(BF16), low.astype(BF16)], axis=0)
        for jj in range(CH // 2):
            lifted = dot(both, pick[:, jj * 256:(jj + 1) * 256])
            lifted = lifted[:ROWS] + lifted[ROWS:]
            for h in range(2):
                j = 2 * jj + h
                mine = jnp.where(
                    up == row16[j:j + 1, :], lifted[:, h * 128:(h + 1) * 128], 0.0
                )
                out[j:j + 1, :] = jnp.sum(mine, axis=0, keepdims=True)

    def put(values):
        high, low = halves(values)
        for j in range(CH):
            at_row = up == row16[j:j + 1, :]
            spread[0:ROWS, j * 128:(j + 1) * 128] = jnp.where(
                at_row, high[j:j + 1, :], 0.0
            ).astype(BF16)
            spread[ROWS:2 * ROWS, j * 128:(j + 1) * 128] = jnp.where(
                at_row, low[j:j + 1, :], 0.0
            ).astype(BF16)
        placed = dot(spread[...], pickt[...])
        return placed[:ROWS] + placed[ROWS:]

    few = lax.broadcasted_iota(jnp.int32, (CH, 128), 0)

    def same_cell(values):
        high, low = halves(values)
        mine = [few == uhi16[j:j + 1, :] for j in range(CH)]
        spread_h = [jnp.where(mine[j], high[j:j + 1, :], 0.0) for j in range(CH)]
        spread_l = [jnp.where(mine[j], low[j:j + 1, :], 0.0) for j in range(CH)]
        both = jnp.concatenate(
            [jnp.concatenate(spread_h, axis=1), jnp.concatenate(spread_l, axis=1)], axis=0
        ).astype(BF16)
        table = dot(both, uone[...])
        table = table[:CH] + table[CH:]
        uhi, ulo = uhi16[...], ulo16[...]
        out = jnp.zeros((CH, 128), F32)
        for r in range(CH):
            row = jnp.broadcast_to(table[r:r + 1, :], (CH, 128))
            found = jnp.take_along_axis(row, ulo, axis=1, mode="promise_in_bounds")
            out = jnp.where(uhi == r, found, out)
        return out

    def send(values, parity):
        for k in range(NB):
            fx[k] = values[4 * k:4 * k + 4, :]
        for m in FAR_FIRST:
            there = peer(m)
            sbuf[m - 1] = fx[kid[there]]
            pltpu.make_async_remote_copy(
                sbuf.at[m - 1], landing[parity].at[m], ssem, rsem.at[parity],
                device_id=(there,), device_id_type=MESH,
            ).start()

    def receive(parity):
        whole = pltpu.make_async_remote_copy(
            sbuf, landing[parity].at[pl.ds(1, NDEV - 1)], ssem, rsem.at[parity],
            device_id=(peer(1),), device_id_type=MESH,
        )
        whole.wait_recv()
        for k in range(NB):
            gx[4 * k:4 * k + 4, :] = landing[parity][at[k]]
        whole.wait_send()

    def wait_all(sent, arrived, size, count, send_sem, recv_sem):
        pltpu.make_async_remote_copy(
            sent.at[pl.ds(size, size * count)], arrived.at[pl.ds(size, size * count)],
            send_sem, recv_sem, device_id=(peer(1),), device_id_type=MESH,
        ).wait()

    def patch(v):
        right = wr[...] * (v - pltpu.roll(v, COLS - 1, 1))
        down = wd[...] * (v - pltpu.roll(v, ROWS - 1, 0))
        return right - pltpu.roll(right, 1, 1) + down - pltpu.roll(down, 1, 0)

    def unfold(ref, c):
        return ref[pl.ds(c, ROWS, stride=4), :]

    def grid(ref):
        return jnp.concatenate([unfold(ref, c) for c in range(4)], axis=1)

    loads[2].wait()
    h = grid(depth)
    take(h, xg)

    pl.semaphore_wait(barrier, NDEV - 1)

    for c in range(PIECES):
        for m in range(1, LOW):
            pltpu.make_async_remote_copy(
                ph1[c].at[pl.ds(0, OWN)], ph1[c].at[pl.ds(m * OWN, OWN)],
                s1.at[c], r1.at[c], device_id=(peer(m),), device_id_type=MESH,
            ).start()
    send(xg[...], 1)

    last_col = lax.broadcasted_iota(jnp.int32, (ROWS, COLS), 1) == COLS - 1
    last_row = lax.broadcasted_iota(jnp.int32, (ROWS, COLS), 0) == ROWS - 1
    wr[...] = jnp.where(last_col, 0.0, 0.5 * (h + pltpu.roll(h, COLS - 1, 1)))
    wd[...] = jnp.where(last_row, 0.0, 0.5 * (h + pltpu.roll(h, ROWS - 1, 0)))
    loads[3].wait()
    mask = grid(wet).astype(F32)
    kw[...] = KAPPA * mask
    take(mask, kwj)
    kwj[...] = KAPPA * kwj[...]
    for load in loads[4:]:
        load.wait()
    wgt[...] = kw[...] * grid(obs)
    take(wgt[...], obj)

    mins[...] = jnp.full((CH * 8, 128), 4096.0, F32)

    def earliest(i, carry):
        mine = row16[pl.ds(i, 1), :] * COLS + col16[pl.ds(i, 1), :]
        column = jnp.transpose(jnp.broadcast_to(mine.astype(F32), (128, 128)))
        number = (up + i * 128).astype(F32)
        for j in range(CH):
            other = (row16[j:j + 1, :] * COLS + col16[j:j + 1, :]).astype(F32)
            found = jnp.where(column == other, number, 4096.0)
            found = jnp.min(found.reshape(16, 8, 128), axis=0)
            mins[8 * j:8 * j + 8, :] = jnp.minimum(mins[8 * j:8 * j + 8, :], found)
        return carry

    lax.fori_loop(0, CH, earliest, 0)
    for j in range(CH):
        u = jnp.min(mins[8 * j:8 * j + 8, :], axis=0, keepdims=True).astype(jnp.int32)
        uhi16[j:j + 1, :] = lax.div(u, 128)
        ulo16[j:j + 1, :] = lax.rem(u, 128)
    for j in range(CH):
        ulo = ulo16[j:j + 1, :]
        column = jnp.transpose(jnp.broadcast_to(ulo.astype(F32), (128, 128)))
        uone[j * 128:(j + 1) * 128, :] = jnp.where(
            column == across.astype(F32), 1.0, 0.0
        ).astype(BF16)
        column = jnp.transpose(
            jnp.broadcast_to(col16[j:j + 1, :].astype(F32), (128, 128))
        )
        for c in range(4):
            pickt[j * 128:(j + 1) * 128, c * 128:(c + 1) * 128] = jnp.where(
                column == (across + c * 128).astype(F32), 1.0, 0.0
            ).astype(BF16)

    place = []
    for j in range(HIGHN):
        for k in range(READS):
            b = reads[k, high_of[j] + my_low]
            owner = lax.div(b, OWN)
            place.append(differ(lax.rem(owner, LOW), my_low, 3) * OWN + lax.rem(b, OWN))
    for c in range(PIECES):
        wait_all(ph1[c], ph1[c], OWN, LOW - 1, s1.at[c], r1.at[c])
        for j in range(HIGHN):
            part = pl.ds(j * READS, READS)
            goal = sb2 if j else rb2
            for k in range(READS):
                goal[c, j * READS + k] = ph1[c][place[j * READS + k]]
            if j:
                pltpu.make_async_remote_copy(
                    sb2.at[c, part], rb2.at[c, part], s2.at[c], r2.at[c],
                    device_id=(high_of[j] + my_low,), device_id_type=MESH,
                ).start()

    receive(1)
    ew[...] = 0.5 * (xg[...] + gx[...])
    dia[...] = put(ew[...])
    for r in range(READS):
        for p in range(2):
            at_row = (2 * r + p) * CH
            uall[at_row:at_row + CH, :] = brows[0, r, pl.ds(p, CH, stride=2), :]
    for c in range(PIECES):
        wait_all(sb2.at[c], rb2.at[c], READS, HIGHN - 1, s2.at[c], r2.at[c])

    lane16 = lax.broadcasted_iota(jnp.int32, (CH, 128), 1)
    zero = jnp.zeros((2 * CH, 128), F32)
    diagonal = []
    for k in range(READS):
        owner = lax.div(reads[k, me], OWN)
        row = differ(lax.div(owner, LOW), my_high, 4)
        block = jnp.concatenate(
            [rb2[c, row * READS + k] for c in range(PIECES)], axis=0
        )
        turned = pltpu.roll(block, 64, 1)
        if k % 2:
            both = [jnp.where(lane16 < 64, 0.0, v) for v in (turned, block)]
        else:
            both = [jnp.where(lane16 < 64, v, 0.0) for v in (block, turned)]
        both = jnp.concatenate(both, axis=0)
        diagonal.append(jnp.concatenate([zero, both] if k > 1 else [both, zero], axis=1))
    uy = bcols[0].reshape(READS * 64, COLS)
    inner = dot(jnp.concatenate(diagonal, axis=0), uy, HIGH)
    bathy = dot(jnp.transpose(uall[...]), inner, HIGH)
    src[...] = kw[...] * grid(sens) * bathy

    bgr[...] = src[...]
    take(src[...], pg)
    gx[...] = jnp.zeros((CH, 128), F32)

    def step(n, parity):
        send(pg[...], parity)
        k = kw[...]
        e = bgr[...] + k * put(gx[...])
        turn = n == TURN
        s = jnp.where(turn, wgt[...] * e, src[...])
        seen[...] = jnp.where(turn, e, seen[...])
        e = jnp.where(turn, s, e)
        src[...] = s
        new = e - k * (patch(e) + dia[...] * e) + s
        bgr[...] = new
        ahead = n == TURN - 1
        take(jnp.where(ahead, wgt[...] * new, new), pg)
        receive(parity)
        x = ew[...] * gx[...]
        gx[...] = x
        scale = jnp.where(ahead, obj[...] * kwj[...], kwj[...])
        pg[...] = pg[...] + scale * same_cell(x)

    def pair(i, carry):
        step(2 * i, 0)
        step(2 * i + 1, 1)
        return carry

    seen[...] = src[...]
    lax.fori_loop(0, TURN, pair, 0)
    last = bgr[...] + kw[...] * put(gx[...])
    seen_obs = grid(obs) * seen[...]
    for c in range(4):
        wobs[pl.ds(c, ROWS, stride=4), :] = seen_obs[:, c * 128:(c + 1) * 128]

    grad = grid(sens) * last
    side = dot(uall[...], grad, HIGH)
    full = lax.dot_general(
        side, bcols[0].reshape(READS * 64, COLS), (((1,), (1,)), ((), ())),
        precision=HIGH, preferred_element_type=F32,
    )
    for r in range(READS):
        half = full[:, (r // 2) * 128:(r // 2 + 1) * 128]
        even = half[2 * r * CH:(2 * r + 1) * CH]
        odd = half[(2 * r + 1) * CH:(2 * r + 2) * CH]
        if r % 2:
            even = pltpu.roll(even, 64, 1)
        else:
            odd = pltpu.roll(odd, 64, 1)
        block = jnp.where(lane16 < 64, even, odd)
        for c in range(PIECES):
            gr[c, r] = block[c * PR:(c + 1) * PR]

    for c in range(PIECES):
        for j in range(1, HIGHN):
            pltpu.make_async_remote_copy(
                gr.at[c, pl.ds(0, READS)], gr.at[c, pl.ds(j * READS, READS)],
                s3.at[c], r3.at[c],
                device_id=(high_of[j] + my_low,), device_id_type=MESH,
            ).start()
    lane = lax.broadcasted_iota(jnp.int32, (1, 128), 1)
    wt[...] = jnp.zeros((128, 128), F32)
    for j in range(HIGHN):
        for k in range(READS):
            s = j * READS + k
            owner = lax.div(reads[k, high_of[j] + my_low], OWN)
            index = jnp.where(lax.div(owner, LOW) == my_high, place[s], -1)
            wt[s:s + 1, :] = jnp.where(lane == index, 1.0, 0.0)
    gather = jnp.transpose(wt[...])[:64, :64]
    for c in range(PIECES):
        wait_all(gr.at[c], gr.at[c], READS, HIGHN - 1, s3.at[c], r3.at[c])
        for i in range(PR):
            sp[c, :, i, :] = dot(gather, gr[c, :, i, :], HIGH)
        for m in range(1, LOW):
            part = pl.ds(m * OWN, OWN)
            pltpu.make_async_remote_copy(
                sp.at[c, part], rp.at[c, part], s4.at[c], r4.at[c],
                device_id=(peer(m),), device_id_type=MESH,
            ).start()
    for c in range(PIECES):
        wait_all(sp.at[c], rp.at[c], OWN, LOW - 1, s4.at[c], r4.at[c])
        total = sp[c, 0:OWN]
        for m in range(1, LOW):
            total = total + rp[c, m * OWN:(m + 1) * OWN]
        acc[c] = total
        for i in range(PR):
            at_lane = (c * PR + i) * 128
            hess[:, at_lane:at_lane + 128] = acc[c, :, i, :]


def on_device(
    control, reads, neighbours, halo_cells, wet_mask, depth, sensitivity, obs_weight,
    basis_rows, basis_cols,
):
    flat = (ROWS * COLS // 128, 128)
    field = pltpu.VMEM((ROWS, COLS), F32)
    few = pltpu.VMEM((CH, 128), F32)
    few_int = pltpu.VMEM((CH, 128), jnp.int32)
    edges = CH * 128
    blocks = pltpu.VMEM((PIECES, LOW * OWN, PR, 128), F32)
    dma = pltpu.SemaphoreType.DMA
    vmem = pl.BlockSpec(memory_space=pltpu.VMEM)
    hess, wobs = pl.pallas_call(
        kernel,
        name="hessian_product",
        out_shape=(
            jax.ShapeDtypeStruct(control.shape, F32),
            jax.ShapeDtypeStruct(flat, F32),
        ),
        in_specs=[pl.BlockSpec(memory_space=pltpu.SMEM)] * 2
        + [pl.BlockSpec(memory_space=pltpu.HBM)] * 8,
        out_specs=(vmem, vmem),
        scratch_shapes=[
            pltpu.VMEM(control.shape, F32),
            pltpu.VMEM(halo_cells.shape, jnp.int32),
            pltpu.VMEM(flat, jnp.int32),
            pltpu.VMEM(flat, F32),
            pltpu.VMEM(flat, F32),
            pltpu.VMEM(flat, F32),
            pltpu.VMEM(basis_rows.shape, F32),
            pltpu.VMEM(basis_cols.shape, F32),
            dma((8,)),
            field, field, field, field, field, field, field,
            few,
            field,
            pltpu.VMEM((COLS, edges), BF16),
            pltpu.VMEM((edges, COLS), BF16),
            pltpu.VMEM((2 * ROWS, edges), BF16),
            pltpu.VMEM((edges, 128), BF16),
            few_int, few_int, few_int, few_int,
            pltpu.VMEM((CH * 8, 128), F32),
            few, few, few, few,
            pltpu.VMEM((NB, 4, 128), F32),
            few,
            pltpu.VMEM((NDEV - 1, 4, 128), F32),
            pltpu.VMEM((NDEV, 4, 128), F32),
            pltpu.VMEM((NDEV, 4, 128), F32),
            *[pltpu.VMEM((LOW * OWN, PR, 128), F32) for _ in range(PIECES)],
            blocks, blocks, blocks, blocks, blocks,
            pltpu.VMEM((128, 128), F32),
            pltpu.VMEM((128, 128), F32),
            pltpu.VMEM((PIECES, OWN, PR, 128), F32),
            pltpu.SMEM((NDEV,), jnp.int32),
            dma, dma((2,)),
            *[dma((PIECES,)) for _ in range(8)],
        ],
        compiler_params=pltpu.CompilerParams(
            collective_id=0, has_side_effects=True, vmem_limit_bytes=63 << 20
        ),
    )(
        reads.T, neighbours.T, control, halo_cells, wet_mask.reshape(flat), depth.reshape(flat),
        sensitivity.reshape(flat), obs_weight.reshape(flat), basis_rows, basis_cols,
    )
    return hess, wobs.reshape(-1)


def solution(mesh):
    return jax.shard_map(
        on_device,
        mesh=mesh,
        in_specs=(
            P("dom", None), P(), P(), P("dom", None, None), P("dom"), P("dom"), P("dom"),
            P("dom"), P("dom", None, None, None), P("dom", None, None, None),
        ),
        out_specs=(P("dom", None), P("dom")),
        check_vma=False,
    )
```

time: 227 us -> 203 us (0.89)
  Pallas kernels: 218 us -> 199 us
  local copies, waits for them, and re-layouts: 7.87 us -> 3.14 us
    pallas_call x1, Pallas kernels: 218 us -> 199 us  [on_device(): pl.pallas_call(kernel, name='hessian_product', out_shape=(jax.ShapeDtypeS...]
    unnamed x18 -> x2, local copies, waits for them, and re-layouts: 7.87 us -> 3.14 us
where the time goes in v2:
time: 203 us; the launch traced here: 202 us
  Pallas kernels  199 us (98%)
  local copies, waits for them, and re-layouts  3.14 us (2%)
    pallas_call x1, Pallas kernels, on_device(): pl.pallas_call(kernel, name='hessian_product', out_shape=(jax.ShapeDtypeS...  199 us

profile of v2, /device:TPU:1, one launch (start us, length us, event | category | flops | bytes accessed | tf_op | source)
XLA Modules:
  0.0 202.3 jit_solution(4641821896298037038)
XLA Ops:
  0.6 198.5 %hessian_product.1 = (f32[8,2048]{1,0:T(8,128)}, f32[512,128]{1,0:T(8,128)}) custom-call(s32[4,128]{1,0:T(4,128)} %bitcast.12, s32[4,128]{1,0:T(4,128)} %bitcast.13, f32[8,2048]{1,0:T(8,128)} %control_hbm.1, s32[1,4,512]{2,1,0:T(4,128)} %cells_hbm.1, s32[512,128]{1,0:T(8,128)} %bitcast.8, f32[512,128]{1,0:T(8,128)} %bitcast.9, f32[512,128]{1,0:T(8,128)} %bitcast.10, ...), custom_call_target="tpu_custom_call" | custom-call | tf_op jit(solution)/shard_map/hessian_product/pallas_call | solution.py:430
  199.2 1.5 copy.14
  200.6 1.7 copy.15

commit v3 on v2

--- a/solution.py
+++ b/solution.py
@@ -71,10 +71,11 @@
 def kernel(
     reads, nbrs, control_hbm, cells_hbm, wet_hbm, depth_hbm, sens_hbm, obs_hbm,
     brows_hbm, bcols_hbm,
-    hess, wobs,
+    hess, wobs_hbm,
+    wobs, outsem,
     control, cells, wet, depth, sens, obs, brows, bcols, insem,
     kw, wr, wd, dia, src, bgr, wgt, obj, seen, pick, pickt, spread, uone,
-    row16, col16, uhi16, ulo16, mins, ew, kwj, xg, gx, fx, pg, sbuf, rbuf0, rbuf1,
+    row16, col16, uhi16, ulo16, mins, ew, kwj, xg, gx, fx, pg, sbuf, rbuf0, rbuf1, rbuf2,
     ph1a, ph1b, ph1c, ph1d, sb2, rb2, gr, sp, rp, wt, uall, acc, kid,
     ssem, rsem, s1, r1, s2, r2, s3, r3, s4, r4,
 ):
@@ -103,9 +104,9 @@
 
     ph1 = (ph1a, ph1b, ph1c, ph1d)
     loads[0].wait()
-    loads[1].wait()
     for i in range(CH):
         ph1[i // PR][0:OWN, i % PR, :] = control[:, i * 128:(i + 1) * 128]
+    loads[1].wait()
     for k in range(NB):
         for c in range(4):
             part = cells[0, k:k + 1, c * 128:(c + 1) * 128]
@@ -120,7 +121,7 @@
         ).astype(BF16)
     nbr = [nbrs[k, me] for k in range(NB)]
     at = [differ(nbr[k], me, 7) for k in range(NB)]
-    landing = (rbuf0, rbuf1)
+    landing = (rbuf0, rbuf1, rbuf2)
     for buf in landing:
         buf[0] = jnp.zeros((4, 128), F32)
 
@@ -177,9 +178,11 @@
             out = jnp.where(uhi == r, found, out)
         return out
 
-    def send(values, parity):
+    def stage(values):
         for k in range(NB):
             fx[k] = values[4 * k:4 * k + 4, :]
+
+    def send(parity):
         for m in FAR_FIRST:
             there = peer(m)
             sbuf[m - 1] = fx[kid[there]]
@@ -196,7 +199,8 @@
         whole.wait_recv()
         for k in range(NB):
             gx[4 * k:4 * k + 4, :] = landing[parity][at[k]]
-        whole.wait_send()
+        if parity < 2:
+            whole.wait_send()
 
     def wait_all(sent, arrived, size, count, send_sem, recv_sem):
         pltpu.make_async_remote_copy(
@@ -219,6 +223,12 @@
     h = grid(depth)
     take(h, xg)
 
+    place = []
+    for j in range(HIGHN):
+        for k in range(READS):
+            b = reads[k, high_of[j] + my_low]
+            owner = lax.div(b, OWN)
+            place.append(differ(lax.rem(owner, LOW), my_low, 3) * OWN + lax.rem(b, OWN))
     pl.semaphore_wait(barrier, NDEV - 1)
 
     for c in range(PIECES):
@@ -227,8 +237,6 @@
                 ph1[c].at[pl.ds(0, OWN)], ph1[c].at[pl.ds(m * OWN, OWN)],
                 s1.at[c], r1.at[c], device_id=(peer(m),), device_id_type=MESH,
             ).start()
-    send(xg[...], 1)
-
     last_col = lax.broadcasted_iota(jnp.int32, (ROWS, COLS), 1) == COLS - 1
     last_row = lax.broadcasted_iota(jnp.int32, (ROWS, COLS), 0) == ROWS - 1
     wr[...] = jnp.where(last_col, 0.0, 0.5 * (h + pltpu.roll(h, COLS - 1, 1)))
@@ -238,6 +246,22 @@
     kw[...] = KAPPA * mask
     take(mask, kwj)
     kwj[...] = KAPPA * kwj[...]
+    for c in range(PIECES):
+        wait_all(ph1[c], ph1[c], OWN, LOW - 1, s1.at[c], r1.at[c])
+        for j in range(HIGHN):
+            part = pl.ds(j * READS, READS)
+            goal = sb2 if j else rb2
+            for k in range(READS):
+                goal[c, j * READS + k] = ph1[c][place[j * READS + k]]
+            if j:
+                pltpu.make_async_remote_copy(
+                    sb2.at[c, part], rb2.at[c, part], s2.at[c], r2.at[c],
+                    device_id=(high_of[j] + my_low,), device_id_type=MESH,
+                ).start()
+
+    stage(xg[...])
+    send(2)
+
     for load in loads[4:]:
         load.wait()
     wgt[...] = kw[...] * grid(obs)
@@ -275,28 +299,10 @@
                 column == (across + c * 128).astype(F32), 1.0, 0.0
             ).astype(BF16)
 
-    place = []
-    for j in range(HIGHN):
-        for k in range(READS):
-            b = reads[k, high_of[j] + my_low]
-            owner = lax.div(b, OWN)
-            place.append(differ(lax.rem(owner, LOW), my_low, 3) * OWN + lax.rem(b, OWN))
-    for c in range(PIECES):
-        wait_all(ph1[c], ph1[c], OWN, LOW - 1, s1.at[c], r1.at[c])
-        for j in range(HIGHN):
-            part = pl.ds(j * READS, READS)
-            goal = sb2 if j else rb2
-            for k in range(READS):
-                goal[c, j * READS + k] = ph1[c][place[j * READS + k]]
-            if j:
-                pltpu.make_async_remote_copy(
-                    sb2.at[c, part], rb2.at[c, part], s2.at[c], r2.at[c],
-                    device_id=(high_of[j] + my_low,), device_id_type=MESH,
-                ).start()
-
-    receive(1)
-    ew[...] = 0.5 * (xg[...] + gx[...])
-    dia[...] = put(ew[...])
+    pltpu.make_async_remote_copy(
+        sbuf, rbuf2.at[pl.ds(1, NDEV - 1)], ssem, rsem.at[2],
+        device_id=(peer(1),), device_id_type=MESH,
+    ).wait_send()
     for r in range(READS):
         for p in range(2):
             at_row = (2 * r + p) * CH
@@ -330,7 +336,16 @@
     gx[...] = jnp.zeros((CH, 128), F32)
 
     def step(n, parity):
-        send(pg[...], parity)
+        stage(pg[...])
+        send(parity)
+        if parity == 0:
+            @pl.when(n == 0)
+            def _():
+                receive(2)
+                ew[...] = 0.5 * (xg[...] + gx[...])
+                dia[...] = put(ew[...])
+                gx[...] = jnp.zeros((CH, 128), F32)
+
         k = kw[...]
         e = bgr[...] + k * put(gx[...])
         turn = n == TURN
@@ -359,6 +374,8 @@
     seen_obs = grid(obs) * seen[...]
     for c in range(4):
         wobs[pl.ds(c, ROWS, stride=4), :] = seen_obs[:, c * 128:(c + 1) * 128]
+    store = pltpu.make_async_copy(wobs, wobs_hbm, outsem)
+    store.start()
 
     grad = grid(sens) * last
     side = dot(uall[...], grad, HIGH)
@@ -394,10 +411,13 @@
             index = jnp.where(lax.div(owner, LOW) == my_high, place[s], -1)
             wt[s:s + 1, :] = jnp.where(lane == index, 1.0, 0.0)
     gather = jnp.transpose(wt[...])[:64, :64]
+    gather = jnp.concatenate([gather, gather], axis=1).astype(BF16)
     for c in range(PIECES):
         wait_all(gr.at[c], gr.at[c], READS, HIGHN - 1, s3.at[c], r3.at[c])
+        wide = jnp.concatenate([gr[c, :, i, :] for i in range(PR)], axis=1)
+        wide = dot(gather, jnp.concatenate(halves(wide), axis=0).astype(BF16))
         for i in range(PR):
-            sp[c, :, i, :] = dot(gather, gr[c, :, i, :], HIGH)
+            sp[c, :, i, :] = wide[:, i * 128:(i + 1) * 128]
         for m in range(1, LOW):
             part = pl.ds(m * OWN, OWN)
             pltpu.make_async_remote_copy(
@@ -413,6 +433,7 @@
         for i in range(PR):
             at_lane = (c * PR + i) * 128
             hess[:, at_lane:at_lane + 128] = acc[c, :, i, :]
+    store.wait()
 
 
 def on_device(
@@ -436,8 +457,10 @@
         ),
         in_specs=[pl.BlockSpec(memory_space=pltpu.SMEM)] * 2
         + [pl.BlockSpec(memory_space=pltpu.HBM)] * 8,
-        out_specs=(vmem, vmem),
+        out_specs=(vmem, pl.BlockSpec(memory_space=pltpu.HBM)),
         scratch_shapes=[
+            pltpu.VMEM(flat, F32),
+            dma,
             pltpu.VMEM(control.shape, F32),
             pltpu.VMEM(halo_cells.shape, jnp.int32),
             pltpu.VMEM(flat, jnp.int32),
@@ -462,13 +485,14 @@
             pltpu.VMEM((NDEV - 1, 4, 128), F32),
             pltpu.VMEM((NDEV, 4, 128), F32),
             pltpu.VMEM((NDEV, 4, 128), F32),
+            pltpu.VMEM((NDEV, 4, 128), F32),
             *[pltpu.VMEM((LOW * OWN, PR, 128), F32) for _ in range(PIECES)],
             blocks, blocks, blocks, blocks, blocks,
             pltpu.VMEM((128, 128), F32),
             pltpu.VMEM((128, 128), F32),
             pltpu.VMEM((PIECES, OWN, PR, 128), F32),
             pltpu.SMEM((NDEV,), jnp.int32),
-            dma, dma((2,)),
+            dma, dma((3,)),
             *[dma((PIECES,)) for _ in range(8)],
         ],
         compiler_params=pltpu.CompilerParams(

time: 203 us -> 201 us (level)
  no operation moved by 1% of the time
where the time goes in v3:
time: 201 us
  Pallas kernels  197 us (98%)
  local copies, waits for them, and re-layouts  3.14 us (2%)
    pallas_call x1, Pallas kernels, on_device(): pl.pallas_call(kernel, name='hessian_product', out_shape=(jax.ShapeDtypeS...  197 us

profile of v3, /device:TPU:1, one launch (start us, length us, event | category | flops | bytes accessed | tf_op | source)
XLA Modules:
  0.0 201.2 jit_solution(6919281868256869733)
XLA Ops:
  0.6 197.4 %hessian_product.1 = (f32[8,2048]{1,0:T(8,128)}, f32[512,128]{1,0:T(8,128)}) custom-call(s32[4,128]{1,0:T(4,128)} %bitcast.12, s32[4,128]{1,0:T(4,128)} %bitcast.13, f32[8,2048]{1,0:T(8,128)} %control_hbm.1, s32[1,4,512]{2,1,0:T(4,128)} %cells_hbm.1, s32[512,128]{1,0:T(8,128)} %bitcast.8, f32[512,128]{1,0:T(8,128)} %bitcast.9, f32[512,128]{1,0:T(8,128)} %bitcast.10, ...), custom_call_target="tpu_custom_call" | custom-call | tf_op jit(solution)/shard_map/hessian_product/pallas_call | solution.py:451
  198.1 1.5 copy.14
  199.5 1.7 copy.15

commit v4 on v3

--- a/solution.py
+++ b/solution.py
@@ -49,6 +49,31 @@
             bit = lax.rem(lax.div(value, 1 << i), 2)
             out = out + (1 - 2 * bit) * (1 << i)
     return out
+
+
+ROLES = (0, 1, 2, 0)
+
+
+def low_mask(axis, t):
+    return (t & 1) | ((t >> 1) << (1 + 2 * axis))
+
+
+def high_mask(axis, j):
+    one, two = [b for b in range(3) if b != axis]
+    return ((j & 3) << (1 + 2 * one)) | ((j >> 2) << (1 + 2 * two))
+
+
+def place_on(axis, d):
+    return lax.rem(lax.div(d, 2 * 4 ** axis), 4)
+
+
+def low_index(axis, d):
+    return lax.rem(d, 2) + 2 * place_on(axis, d)
+
+
+def high_index(axis, d):
+    one, two = [b for b in range(3) if b != axis]
+    return place_on(one, d) + 4 * place_on(two, d)
 
 
 def differ(a, b, bits):
@@ -223,19 +248,22 @@
     h = grid(depth)
     take(h, xg)
 
-    place = []
-    for j in range(HIGHN):
-        for k in range(READS):
-            b = reads[k, high_of[j] + my_low]
-            owner = lax.div(b, OWN)
-            place.append(differ(lax.rem(owner, LOW), my_low, 3) * OWN + lax.rem(b, OWN))
+    place = [[], [], []]
+    for axis in range(3):
+        for j in range(HIGHN):
+            for k in range(READS):
+                b = reads[k, peer(high_mask(axis, j))]
+                owner = lax.div(b, OWN)
+                index = differ(low_index(axis, owner), low_index(axis, me), 3)
+                place[axis].append(index * OWN + lax.rem(b, OWN))
     pl.semaphore_wait(barrier, NDEV - 1)
 
     for c in range(PIECES):
         for m in range(1, LOW):
             pltpu.make_async_remote_copy(
                 ph1[c].at[pl.ds(0, OWN)], ph1[c].at[pl.ds(m * OWN, OWN)],
-                s1.at[c], r1.at[c], device_id=(peer(m),), device_id_type=MESH,
+                s1.at[c], r1.at[c], device_id=(peer(low_mask(ROLES[c], m)),),
+                device_id_type=MESH,
             ).start()
     last_col = lax.broadcasted_iota(jnp.int32, (ROWS, COLS), 1) == COLS - 1
     last_row = lax.broadcasted_iota(jnp.int32, (ROWS, COLS), 0) == ROWS - 1
@@ -252,11 +280,11 @@
             part = pl.ds(j * READS, READS)
             goal = sb2 if j else rb2
             for k in range(READS):
-                goal[c, j * READS + k] = ph1[c][place[j * READS + k]]
+                goal[c, j * READS + k] = ph1[c][place[ROLES[c]][j * READS + k]]
             if j:
                 pltpu.make_async_remote_copy(
                     sb2.at[c, part], rb2.at[c, part], s2.at[c], r2.at[c],
-                    device_id=(high_of[j] + my_low,), device_id_type=MESH,
+                    device_id=(peer(high_mask(ROLES[c], j)),), device_id_type=MESH,
                 ).start()
 
     stage(xg[...])
@@ -315,9 +343,9 @@
     diagonal = []
     for k in range(READS):
         owner = lax.div(reads[k, me], OWN)
-        row = differ(lax.div(owner, LOW), my_high, 4)
+        row = [differ(high_index(x, owner), high_index(x, me), 4) for x in range(3)]
         block = jnp.concatenate(
-            [rb2[c, row * READS + k] for c in range(PIECES)], axis=0
+            [rb2[c, row[ROLES[c]] * READS + k] for c in range(PIECES)], axis=0
         )
         turned = pltpu.roll(block, 64, 1)
         if k % 2:
@@ -400,29 +428,32 @@
             pltpu.make_async_remote_copy(
                 gr.at[c, pl.ds(0, READS)], gr.at[c, pl.ds(j * READS, READS)],
                 s3.at[c], r3.at[c],
-                device_id=(high_of[j] + my_low,), device_id_type=MESH,
+                device_id=(peer(high_mask(ROLES[c], j)),), device_id_type=MESH,
             ).start()
     lane = lax.broadcasted_iota(jnp.int32, (1, 128), 1)
-    wt[...] = jnp.zeros((128, 128), F32)
-    for j in range(HIGHN):
-        for k in range(READS):
-            s = j * READS + k
-            owner = lax.div(reads[k, high_of[j] + my_low], OWN)
-            index = jnp.where(lax.div(owner, LOW) == my_high, place[s], -1)
-            wt[s:s + 1, :] = jnp.where(lane == index, 1.0, 0.0)
-    gather = jnp.transpose(wt[...])[:64, :64]
-    gather = jnp.concatenate([gather, gather], axis=1).astype(BF16)
+    gather = []
+    for axis in range(3):
+        wt[...] = jnp.zeros((128, 128), F32)
+        for j in range(HIGHN):
+            for k in range(READS):
+                s = j * READS + k
+                owner = lax.div(reads[k, peer(high_mask(axis, j))], OWN)
+                mine = high_index(axis, owner) == high_index(axis, me)
+                index = jnp.where(mine, place[axis][s], -1)
+                wt[s:s + 1, :] = jnp.where(lane == index, 1.0, 0.0)
+        turned = jnp.transpose(wt[...])[:64, :64]
+        gather.append(jnp.concatenate([turned, turned], axis=1).astype(BF16))
     for c in range(PIECES):
         wait_all(gr.at[c], gr.at[c], READS, HIGHN - 1, s3.at[c], r3.at[c])
         wide = jnp.concatenate([gr[c, :, i, :] for i in range(PR)], axis=1)
-        wide = dot(gather, jnp.concatenate(halves(wide), axis=0).astype(BF16))
+        wide = dot(gather[ROLES[c]], jnp.concatenate(halves(wide), axis=0).astype(BF16))
         for i in range(PR):
             sp[c, :, i, :] = wide[:, i * 128:(i + 1) * 128]
         for m in range(1, LOW):
             part = pl.ds(m * OWN, OWN)
             pltpu.make_async_remote_copy(
                 sp.at[c, part], rp.at[c, part], s4.at[c], r4.at[c],
-                device_id=(peer(m),), device_id_type=MESH,
+                device_id=(peer(low_mask(ROLES[c], m)),), device_id_type=MESH,
             ).start()
     for c in range(PIECES):
         wait_all(sp.at[c], rp.at[c], OWN, LOW - 1, s4.at[c], r4.at[c])

time: 201 us -> 200 us (level)
  no operation moved by 1% of the time
where the time goes in v4:
time: 200 us
  Pallas kernels  196 us (98%)
  local copies, waits for them, and re-layouts  3.14 us (2%)
    pallas_call x1, Pallas kernels, on_device(): pl.pallas_call(kernel, name='hessian_product', out_shape=(jax.ShapeDtypeS...  196 us

profile of v4, /device:TPU:1, one launch (start us, length us, event | category | flops | bytes accessed | tf_op | source)
XLA Modules:
  0.0 199.8 jit_solution(11281174726157882269)
XLA Ops:
  0.6 196.0 %hessian_product.1 = (f32[8,2048]{1,0:T(8,128)}, f32[512,128]{1,0:T(8,128)}) custom-call(s32[4,128]{1,0:T(4,128)} %bitcast.12, s32[4,128]{1,0:T(4,128)} %bitcast.13, f32[8,2048]{1,0:T(8,128)} %control_hbm.1, s32[1,4,512]{2,1,0:T(4,128)} %cells_hbm.1, s32[512,128]{1,0:T(8,128)} %bitcast.8, f32[512,128]{1,0:T(8,128)} %bitcast.9, f32[512,128]{1,0:T(8,128)} %bitcast.10, ...), custom_call_target="tpu_custom_call" | custom-call | tf_op jit(solution)/shard_map/hessian_product/pallas_call | solution.py:482
  196.6 1.5 copy.14
  198.1 1.7 copy.15
